TPU v7x, 512 devices: a whole 4x8x8 slice. The times are simulated.
512 devices in a mesh: dp: 16 (over x, y_lo, core), mp: 32 (over z, y_hi).
Axes of the slice: x: 4, y: 8 (y_hi: 4, y_lo: 2; y = y_hi * 2 + y_lo), z: 8, core: 2. Of those that a mesh axis runs over, the one named last changes fastest.
Arguments:
- tokens: bfloat16 [256, 4608], P('mp', 'dp'), may hold values from -6 to 6
- gate_weight: bfloat16 [4608, 36864], P('dp', 'mp'), may hold values from -0.09375 to 0.09375
- up_weight: bfloat16 [4608, 36864], P('dp', 'mp'), may hold values from -0.09375 to 0.09375
- down_weight: bfloat16 [36864, 4608], P('mp', 'dp'), may hold values from -0.03125 to 0.03125
- cotangent: bfloat16 [256, 4608], P('mp', 'dp'), may hold values from -6 to 6
Outputs:
- layer_out: float32 [256, 4608], P('mp', 'dp')
- grad_input: float32 [256, 4608], P('mp', 'dp')
- grad_gate_w: bfloat16 [4608, 36864], P('dp', 'mp')
- grad_up_w: bfloat16 [4608, 36864], P('dp', 'mp')
- grad_down_w: bfloat16 [36864, 4608], P('mp', 'dp')
All inputs are finite; a program needn't handle non-finite values.
Results may differ from a plain program's by a relative error of at most 0.0049.
Values may be sent and summed in bfloat16 or wider, within the bound.
A program may use at most 64 MiB of HBM per device.

v0:
```python
import jax
import jax.numpy as jnp
from jax import lax
from jax.sharding import PartitionSpec as P

GELU_SCALE = 0.7978845608028654
CUBIC_TERM = 0.044715
ROWS_DIMS = (((0,), (0,)), ((), ()))
COLS_DIMS = (((1,), (1,)), ((), ()))


def gelu_parts(values):
    tanh_part = jnp.tanh(GELU_SCALE * (values + CUBIC_TERM * values * values * values))
    gelu_value = 0.5 * values * (1.0 + tanh_part)
    gelu_slope = 0.5 * (1.0 + tanh_part) + 0.5 * values * (
        1.0 - tanh_part * tanh_part
    ) * GELU_SCALE * (1.0 + 3.0 * CUBIC_TERM * values * values)
    return (gelu_value, gelu_slope)


def local(tokens, gate_weight, up_weight, down_weight, cotangent):
    inputs, cot_rows = (
        lax.all_gather(tokens, "mp", axis=0, tiled=True),
        lax.all_gather(cotangent, "mp", axis=0, tiled=True),
    )
    unit_count = gate_weight.shape[1]
    row_block = inputs
    gate_part = jnp.dot(row_block, gate_weight, preferred_element_type=jnp.float32)
    up_part = jnp.dot(row_block, up_weight, preferred_element_type=jnp.float32)
    unit_sums = lax.psum_scatter(
        jnp.concatenate([gate_part, up_part], axis=1), "dp", scatter_dimension=0, tiled=True
    )
    gelu_value, gelu_slope = gelu_parts(unit_sums[:, :unit_count])
    up_sums = unit_sums[:, unit_count:]
    hidden_own = (gelu_value * up_sums).astype(jnp.bfloat16)
    hidden_all = lax.all_gather(hidden_own, "dp", axis=0, tiled=True)
    row_block = cot_rows
    grad_hidden = lax.psum_scatter(
        lax.dot_general(row_block, down_weight, COLS_DIMS, preferred_element_type=jnp.float32),
        "dp",
        scatter_dimension=0,
        tiled=True,
    )
    own_gate = (grad_hidden * up_sums * gelu_slope).astype(jnp.bfloat16)
    own_up = (grad_hidden * gelu_value).astype(jnp.bfloat16)
    grad_gate, grad_up = (
        lax.all_gather(own_gate, "dp", axis=0, tiled=True),
        lax.all_gather(own_up, "dp", axis=0, tiled=True),
    )
    row_block = hidden_all
    layer_out = lax.psum_scatter(
        jnp.dot(row_block, down_weight, preferred_element_type=jnp.float32),
        "mp",
        scatter_dimension=0,
        tiled=True,
    )
    grad_down_w = lax.dot_general(
        hidden_all, cot_rows, ROWS_DIMS, preferred_element_type=jnp.float32
    ).astype(jnp.bfloat16)
    grad_gate_w = lax.dot_general(
        inputs, grad_gate, ROWS_DIMS, preferred_element_type=jnp.float32
    ).astype(jnp.bfloat16)
    grad_up_w = lax.dot_general(
        inputs, grad_up, ROWS_DIMS, preferred_element_type=jnp.float32
    ).astype(jnp.bfloat16)
    gate_back = lax.dot_general(
        grad_gate, gate_weight, COLS_DIMS, preferred_element_type=jnp.float32
    )
    up_back = lax.dot_general(grad_up, up_weight, COLS_DIMS, preferred_element_type=jnp.float32)
    grad_input = lax.psum_scatter(gate_back + up_back, "mp", scatter_dimension=0, tiled=True)
    return (layer_out, grad_input, grad_gate_w, grad_up_w, grad_down_w)


def solution(mesh):
    return jax.shard_map(
        local,
        mesh=mesh,
        in_specs=(P("mp", "dp"), P("dp", "mp"), P("dp", "mp"), P("mp", "dp"), P("mp", "dp")),
        out_specs=(P("mp", "dp"), P("mp", "dp"), P("dp", "mp"), P("dp", "mp"), P("mp", "dp")),
        check_vma=False,
    )
```

profile of v0, /device:TPU:2, one launch (start us, length us, event | category | flops | bytes accessed | tf_op | source)
XLA Modules:
  0.0 631.1 jit_solution(17181573657319591406)
XLA Ops:
  7.2 0.0 copy-start
  7.2 0.0 reduce-scatter.5.cloned.1.call-start
  7.2 89.4 %all_gather.17 = bf16[256,288]{1,0:T(8,128)(2,1)S(1)} all-gather(bf16[8,288]{1,0:T(8,128)(2,1)} %param.9), channel_id=1, replica_groups=mesh['dp'=16,'mp'=32] {'mp'}, dimensions={0}, use_global_device_ids=true | all-gather | bytes 152064 | tf_op jit(solution)/shard_map/all_gather | solution.py:24
  96.6 0.0 copy-start.3
  96.6 2.6 fusion.12
  99.2 0.0 copy-start.2
  99.2 0.0 reduce-scatter.5.cloned.1.call-update
  99.2 0.0 reduce-scatter.3.cloned.1.call-start
  99.3 0.0 copy-done.3
  99.3 76.6 %all_gather.15 = bf16[256,288]{1,0:T(8,128)(2,1)S(1)} all-gather(bf16[8,288]{1,0:T(8,128)(2,1)S(1)} %copy-done.3), channel_id=1, replica_groups=mesh['dp'=16,'mp'=32] {'mp'}, dimensions={0}, use_global_device_ids=true | all-gather | bytes 152064 | tf_op jit(solution)/shard_map/all_gather | solution.py:23
  175.9 0.0 copy-done.2
  175.9 0.5 fusion.10
  176.4 0.0 copy-done
  176.4 0.5 fusion.9
  176.9 1.6 pad_maximum_fusion
  178.4 0.0 reduce-scatter.3.cloned.1.call-update
  178.5 0.0 all-reduce.5.cloned.1.call-start
  178.5 1.3 dynamic-slice
  180.4 0.0 reduce-scatter.5.cloned.1.call-done
  180.5 54.9 %reduce-scatter.3.cloned.1.call-done = f32[16,2304]{1,0:T(8,128)} async-done(((f32[256,2304]{1,0:T(8,128)}), f32[16,2304]{1,0:T(8,128)}) %reduce-scatter.3.cloned.1.call-update) | async-done | bytes 147472 | tf_op jit(solution)/shard_map/reduce_scatter | solution.py:30
  235.4 1.0 multiply_convert_fusion
  236.4 23.7 %all_gather.18 = bf16[256,1152]{1,0:T(8,128)(2,1)S(1)} all-gather(bf16[16,1152]{1,0:T(8,128)(2,1)S(1)} %get-tuple-element.8), channel_id=1, replica_groups=mesh['dp'=16,'mp'=32] {'dp'}, dimensions={0}, use_global_device_ids=true | all-gather | bytes 626688 | tf_op jit(solution)/shard_map/all_gather | solution.py:47
  260.1 0.0 copy-start.1
  260.1 0.5 fusion.13
  260.6 19.9 %all_gather.19 = bf16[256,1152]{1,0:T(8,128)(2,1)S(1)} all-gather(bf16[16,1152]{1,0:T(8,128)(2,1)S(1)} %get-tuple-element.7), channel_id=1, replica_groups=mesh['dp'=16,'mp'=32] {'dp'}, dimensions={0}, use_global_device_ids=true | all-gather | bytes 626688 | tf_op jit(solution)/shard_map/all_gather | solution.py:48
  280.5 19.6 %all_gather.16 = bf16[256,1152]{1,0:T(8,128)(2,1)S(1)} all-gather(bf16[16,1152]{1,0:T(8,128)(2,1)S(1)} %get-tuple-element.9), channel_id=1, replica_groups=mesh['dp'=16,'mp'=32] {'dp'}, dimensions={0}, use_global_device_ids=true | all-gather | bytes 626688 | tf_op jit(solution)/shard_map/all_gather | solution.py:36
  300.1 0.0 copy-done.1
  300.1 1.3 fusion.11
  301.4 1.3 convolution_add_fusion
  302.6 0.0 all-reduce.5.cloned.1.call-update
  302.7 1.2 fusion
  303.9 1.2 fusion.1
  305.2 1.2 convolution_convert_fusion
  306.4 316.8 %all-reduce.5.cloned.1.call-done = (f32[256,288]{1,0:T(8,128)}, f32[256,288]{1,0:T(8,128)}) async-done(((f32[256,288]{1,0:T(8,128)}, f32[256,288]{1,0:T(8,128)}), (f32[256,288]{1,0:T(8,128)}, f32[256,288]{1,0:T(8,128)})) %all-reduce.5.cloned.1.call-update) | async-done | bytes 589840
  623.2 1.3 constant_dynamic-slice_fusion
Async XLA Ops:
  7.2 169.2 %copy-start = (bf16[288,1152]{1,0:T(8,128)(2,1)S(1)}, bf16[288,1152]{1,0:T(8,128)(2,1)}, u32[]{:S(2)}) copy-start(bf16[288,1152]{1,0:T(8,128)(2,1)} %param.6) | copy-start | bytes 1990660
  7.2 173.3 %reduce-scatter.5.cloned.1.call-start = ((), (), s32[]{:S(2)}) async-start(), calls=%async_computation.3 | async-start | bytes 1253376 | tf_op jit(solution)/shard_map/reduce_scatter | solution.py:38
  96.6 2.7 copy-start.3
  99.2 76.7 %copy-start.2 = (bf16[288,1152]{1,0:T(8,128)(2,1)S(1)}, bf16[288,1152]{1,0:T(8,128)(2,1)}, u32[]{:S(2)}) copy-start(bf16[288,1152]{1,0:T(8,128)(2,1)} %param.7) | copy-start | bytes 1990660
  99.2 136.1 %reduce-scatter.3.cloned.1.call-start = ((), (), s32[]{:S(2)}) async-start(), calls=%async_computation.2 | async-start | bytes 2506752 | tf_op jit(solution)/shard_map/reduce_scatter | solution.py:30
  178.5 444.7 %all-reduce.5.cloned.1.call-start = ((), (), s32[]{:S(2)}) async-start(), calls=%async_computation.4 | async-start | bytes 1572864
  260.1 40.0 %copy-start.1 = (bf16[1152,288]{0,1:T(8,128)(2,1)S(1)}, bf16[1152,288]{0,1:T(8,128)(2,1)}, u32[]{:S(2)}) copy-start(bf16[1152,288]{0,1:T(8,128)(2,1)} %param.8) | copy-start | bytes 1990660
Sparse Core Ops, SparseCore 0:
  99.4 52.0 reduce-scatter.4
  178.6 56.7 reduce-scatter.2
  302.8 320.3 all-reduce.4
where the time goes:
time: 631 us
  waiting for transfers between devices  372 us (59%)
  blocking collectives  229 us (36%)
  between operations  14.5 us (2%)
  matrix products  10.3 us (2%)
    unnamed x4, waiting for transfers between devices  317 us
    all_gather x1, blocking collectives, local(): lax.all_gather(cotangent, 'mp', axis=0, tiled=True)  89.4 us
    all_gather x1, blocking collectives, local(): lax.all_gather(tokens, 'mp', axis=0, tiled=True)  76.6 us
    reduce_scatter x1, waiting for transfers between devices, local(): lax.psum_scatter(jnp.concatenate([gate_part, up_part], axis=1), 'dp', sca...  54.9 us
    all_gather x1, blocking collectives, local(): lax.all_gather(own_gate, 'dp', axis=0, tiled=True)  23.7 us
    all_gather x1, blocking collectives, local(): lax.all_gather(own_up, 'dp', axis=0, tiled=True)  19.9 us
    all_gather x1, blocking collectives, local(): hidden_all = lax.all_gather(hidden_own, 'dp', axis=0, tiled=True)  19.6 us
  transfers between devices with their start and end apart: 3, of which 2 were waited for; matrix products, arithmetic and copies ran while one was open for 1% of the time, Pallas kernels for 0%

commit v1 on v0

v1 whole, which is shorter than its diff:
```python
import functools

import jax
import jax.numpy as jnp
from jax import lax
from jax.experimental import pallas as pl
from jax.experimental.pallas import tpu as pltpu
from jax.sharding import PartitionSpec as P

GELU_SCALE = 0.7978845608028654
CUBIC_TERM = 0.044715
ROWS_DIMS = (((0,), (0,)), ((), ()))
COLS_DIMS = (((1,), (1,)), ((), ()))
MESH_ID = pl.DeviceIdType.MESH
F32 = jnp.float32
BF16 = jnp.bfloat16


def gelu_parts(values):
    tanh_part = jnp.tanh(GELU_SCALE * (values + CUBIC_TERM * values * values * values))
    gelu_value = 0.5 * values * (1.0 + tanh_part)
    gelu_slope = 0.5 * (1.0 + tanh_part) + 0.5 * values * (
        1.0 - tanh_part * tanh_part
    ) * GELU_SCALE * (1.0 + 3.0 * CUBIC_TERM * values * values)
    return (gelu_value, gelu_slope)


def total_of(ref, n):
    total = ref[0].astype(F32)
    for i in range(1, n):
        total += ref[i].astype(F32)
    return total


def kernel(
    sizes,
    tok, cot, gate_h, up_h, down_h,
    lo_o, gi_o, ggw_o, guw_o, gdw_o,
    GU, DN, WB, DB, XO, XS, TK, CT, CS, PB, GB, RP, RG, HB,
    AZ, RZ, AY, RY, BY, SY, BZ, SZ, ggw_v, guw_v, gdw_v,
    ld_sem, wx_s, wx_r, p1_s, p1_r, xs_s, xs_r, rp_s, rp_r, rg_s, rg_r,
    ag_s, ag_r, fw_s, fw_r, a_s, a_r, b_s, b_r, out_sem,
):
    NQ, NZ, NY = sizes
    MP = NZ * NY
    dp = lax.axis_index("dp")
    mp = lax.axis_index("mp")
    c = lax.rem(dp, 2)
    oc = 1 - c
    q = lax.div(dp, 2)
    sib = dp + 1 - 2 * c
    z = lax.div(mp, NY)
    y = lax.rem(mp, NY)

    def rcopy(src, dst, ssem, rsem, to_dp, to_mp):
        return pltpu.make_async_remote_copy(
            src_ref=src, dst_ref=dst, send_sem=ssem, recv_sem=rsem,
            device_id=(to_dp, to_mp), device_id_type=MESH_ID,
        )

    def ahead(i, k, n):
        return lax.rem(i + k, n)

    loads = [
        pltpu.make_async_copy(gate_h, GU.at[0], ld_sem.at[0]),
        pltpu.make_async_copy(up_h, GU.at[1], ld_sem.at[1]),
        pltpu.make_async_copy(down_h, DN, ld_sem.at[2]),
    ]
    for copy in loads:
        copy.start()

    barrier = pltpu.get_barrier_semaphore()
    partners = [(sib, mp)]
    for k in range(1, NQ):
        partners.append((2 * ahead(q, k, NQ) + c, mp))
        partners.append((2 * ahead(q, k, NQ) + oc, mp))
    for k in range(1, MP):
        partners.append((dp, ahead(mp, k, MP)))
    for partner in partners:
        pl.semaphore_signal(barrier, inc=1, device_id=partner, device_id_type=MESH_ID)
    XO[mp] = jnp.concatenate([tok[...].astype(F32), cot[...].astype(F32)], axis=0).astype(BF16)
    pl.semaphore_wait(barrier, len(partners))

    p1 = []
    for k in range(1, MP):
        copy = rcopy(XO.at[mp], XO.at[mp], p1_s.at[k], p1_r.at[k], dp, ahead(mp, k, MP))
        copy.start()
        p1.append(copy)
    for copy in loads:
        copy.wait()
    wx = [
        rcopy(GU.at[oc], WB, wx_s.at[0], wx_r.at[0], sib, mp),
        rcopy(DN, DB, wx_s.at[1], wx_r.at[1], sib, mp),
    ]
    for copy in wx:
        copy.start()
    for copy in p1:
        copy.wait_recv()
    xs = rcopy(XO, XS, xs_s, xs_r, sib, mp)
    xs.start()

    def rows_of(ref):
        both = ref[...].astype(F32)
        rows, feats = both.shape[1] // 2, both.shape[2]
        both = both.reshape(MP, 2, rows, feats)
        return (
            both[:, 0].reshape(MP * rows, feats).astype(BF16),
            both[:, 1].reshape(MP * rows, feats).astype(BF16),
        )

    t_own, c_own = rows_of(XO)
    TK[...] = t_own
    CT[...] = c_own.reshape(CT.shape)
    acc = jnp.dot(t_own, GU[c], preferred_element_type=F32)
    for copy in wx:
        copy.wait_recv()
    xs.wait_recv()
    t_sib, c_sib = rows_of(XS)
    CS[...] = c_sib.reshape(CS.shape)
    acc += jnp.dot(t_sib, WB[...], preferred_element_type=F32)
    PB[...] = acc.astype(BF16).reshape(PB.shape)
    rp = []
    for k in range(NQ):
        for cc in range(2):
            if k == 0 and cc == 0:
                continue
            to = 2 * ahead(q, k, NQ) + (oc if cc else c)
            i = 2 * k + cc
            copy = rcopy(PB.at[to], RP.at[c, q], rp_s.at[i], rp_r.at[i], to, mp)
            copy.start()
            rp.append(copy)
    RP[c, q] = PB[dp]

    half = CT.shape[0] * CT.shape[2]
    feats = CT.shape[3]
    acc = lax.dot_general(
        CT[:, pl.ds(c, 1)].reshape(half, feats), DN[...], COLS_DIMS, preferred_element_type=F32
    ) + lax.dot_general(
        CS[:, pl.ds(c, 1)].reshape(half, feats), DB[...], COLS_DIMS, preferred_element_type=F32
    )
    GB[...] = acc.astype(BF16).reshape(GB.shape)
    rg = []
    for k in range(1, NQ):
        to = ahead(q, k, NQ)
        copy = rcopy(GB.at[to], RG.at[q], rg_s.at[k], rg_r.at[k], 2 * to + c, mp)
        copy.start()
        rg.append(copy)
    RG[q] = GB[q]

    for copy in rp:
        copy.wait_recv()
    g_sum = total_of(RP.at[0], NQ)
    u_sum = total_of(RP.at[1], NQ)
    gelu_value, gelu_slope = gelu_parts(g_sum)
    HB[dp, 0] = (gelu_value * u_sum).astype(BF16)
    for copy in rg:
        copy.wait_recv()
    gh_sum = total_of(RG, NQ)
    HB[dp, 1] = (gh_sum * u_sum * gelu_slope).astype(BF16)
    HB[dp, 2] = (gh_sum * gelu_value).astype(BF16)

    ag = []
    for k in range(1, NQ):
        copy = rcopy(HB.at[dp], HB.at[dp], ag_s.at[k], ag_r.at[k], 2 * ahead(q, k, NQ) + c, mp)
        copy.start()
        ag.append(copy)
    fw = [rcopy(HB.at[dp], HB.at[dp], fw_s.at[0], fw_r.at[0], sib, mp)]
    fw[0].start()
    for k in range(1, NQ):
        ag[k - 1].wait_recv()
        slot = HB.at[2 * ahead(q, NQ - k, NQ) + c]
        copy = rcopy(slot, slot, fw_s.at[k], fw_r.at[k], sib, mp)
        copy.start()
        fw.append(copy)
    for copy in fw:
        copy.wait_recv()

    tokens_n = TK.shape[0]
    units = HB.shape[3]

    def gathered(i):
        return HB[:, i].reshape(tokens_n, units)

    rows = lo_o.shape[0]
    lo = jnp.dot(gathered(0), DN[...], preferred_element_type=F32)
    AZ[...] = lo.astype(BF16).reshape(AZ.shape)
    az = []
    for k in range(1, NZ):
        to = ahead(z, k, NZ)
        copy = rcopy(AZ.at[to], RZ.at[z], a_s.at[k], a_r.at[k], dp, to * NY + y)
        copy.start()
        az.append(copy)
    RZ[z] = AZ[z]
    gi = lax.dot_general(gathered(1), GU[0], COLS_DIMS, preferred_element_type=F32)
    gi += lax.dot_general(gathered(2), GU[1], COLS_DIMS, preferred_element_type=F32)
    gi = gi.reshape(NZ, NY, rows, feats)
    for i in range(NY):
        AY[i] = gi[:, i].reshape(NZ * rows, feats).astype(BF16)
    ay = []
    for k in range(1, NY):
        to = ahead(y, k, NY)
        copy = rcopy(AY.at[to], RY.at[y], a_s.at[NZ + k], a_r.at[NZ + k], dp, z * NY + to)
        copy.start()
        ay.append(copy)
    RY[y] = AY[y]

    cts = CT[...].reshape(tokens_n, feats)
    gdw_v[...] = lax.dot_general(
        gathered(0), cts, ROWS_DIMS, preferred_element_type=F32
    ).astype(BF16)
    outs = [pltpu.make_async_copy(gdw_v, gdw_o, out_sem.at[0])]
    outs[0].start()

    for copy in az:
        copy.wait_recv()
    BY[...] = total_of(RZ, NZ).reshape(BY.shape)
    by = []
    for k in range(1, NY):
        to = ahead(y, k, NY)
        copy = rcopy(BY.at[to], SY.at[y], b_s.at[k], b_r.at[k], dp, z * NY + to)
        copy.start()
        by.append(copy)
    SY[y] = BY[y]
    for copy in ay:
        copy.wait_recv()
    BZ[...] = total_of(RY, NY).reshape(BZ.shape)
    bz = []
    for k in range(1, NZ):
        to = ahead(z, k, NZ)
        copy = rcopy(BZ.at[to], SZ.at[z], b_s.at[NY + k], b_r.at[NY + k], dp, to * NY + y)
        copy.start()
        bz.append(copy)
    SZ[z] = BZ[z]

    ggw_v[...] = lax.dot_general(
        TK[...], gathered(1), ROWS_DIMS, preferred_element_type=F32
    ).astype(BF16)
    outs.append(pltpu.make_async_copy(ggw_v, ggw_o, out_sem.at[1]))
    outs[1].start()
    guw_v[...] = lax.dot_general(
        TK[...], gathered(2), ROWS_DIMS, preferred_element_type=F32
    ).astype(BF16)
    outs.append(pltpu.make_async_copy(guw_v, guw_o, out_sem.at[2]))
    outs[2].start()

    for copy in by:
        copy.wait_recv()
    lo_o[...] = total_of(SY, NY)
    for copy in bz:
        copy.wait_recv()
    gi_o[...] = total_of(SZ, NZ)

    for copy in p1 + wx + [xs] + rp + rg + ag + fw + az + ay + by + bz:
        copy.wait_send()
    for copy in outs:
        copy.wait()


def solution(mesh):
    dp_n, mp_n = mesh.shape["dp"], mesh.shape["mp"]
    NQ, NY = dp_n // 2, min(4, mp_n // 2)
    NZ = mp_n // NY

    def local(tokens, gate_weight, up_weight, down_weight, cotangent):
        rows, F = tokens.shape
        U = gate_weight.shape[1]
        T = rows * mp_n
        R = T // dp_n
        dma = pltpu.SemaphoreType.DMA
        vmem = pl.BlockSpec(memory_space=pltpu.VMEM)
        hbm = pl.BlockSpec(memory_space=pl.ANY)
        scratch = [
            ((2, F, U), BF16), ((U, F), BF16), ((F, U), BF16), ((U, F), BF16),
            ((mp_n, 2 * rows, F), BF16), ((mp_n, 2 * rows, F), BF16),
            ((T, F), BF16), ((NQ, 2, R, F), BF16), ((NQ, 2, R, F), BF16),
            ((dp_n, R, U), BF16), ((NQ, R, U), BF16),
            ((2, NQ, R, U), BF16), ((NQ, R, U), BF16), ((dp_n, 3, R, U), BF16),
            ((NZ, NY * rows, F), BF16), ((NZ, NY * rows, F), BF16),
            ((NY, NZ * rows, F), BF16), ((NY, NZ * rows, F), BF16),
            ((NY, rows, F), F32), ((NY, rows, F), F32),
            ((NZ, rows, F), F32), ((NZ, rows, F), F32),
            ((F, U), BF16), ((F, U), BF16), ((U, F), BF16),
        ]
        sems = [3, 2, 2, mp_n, mp_n, None, None, dp_n, dp_n, NQ, NQ, NQ, NQ, NQ, NQ,
                NZ + NY, NZ + NY, NZ + NY, NZ + NY, 3]
        return pl.pallas_call(
            functools.partial(kernel, (NQ, NZ, NY)),
            out_shape=(
                jax.ShapeDtypeStruct((rows, F), F32), jax.ShapeDtypeStruct((rows, F), F32),
                jax.ShapeDtypeStruct((F, U), BF16), jax.ShapeDtypeStruct((F, U), BF16),
                jax.ShapeDtypeStruct((U, F), BF16),
            ),
            in_specs=[vmem, vmem, hbm, hbm, hbm],
            out_specs=(vmem, vmem, hbm, hbm, hbm),
            scratch_shapes=[pltpu.VMEM(s, t) for s, t in scratch]
            + [dma if n is None else dma((n,)) for n in sems],
            compiler_params=pltpu.CompilerParams(
                collective_id=0, has_side_effects=True, vmem_limit_bytes=56 * 1024 * 1024
            ),
        )(tokens, cotangent, gate_weight, up_weight, down_weight)

    return jax.shard_map(
        local,
        mesh=mesh,
        in_specs=(P("mp", "dp"), P("dp", "mp"), P("dp", "mp"), P("mp", "dp"), P("mp", "dp")),
        out_specs=(P("mp", "dp"), P("mp", "dp"), P("dp", "mp"), P("dp", "mp"), P("mp", "dp")),
        check_vma=False,
    )
```

time: 631 us -> 83.7 us (0.13)
  the two profiles are of different devices: /device:TPU:2 before, /device:TPU:1 now
where the time goes in v1:
time: 83.7 us; the launch traced here: 83.3 us
  Pallas kernels  74.5 us (89%)
  local copies, waits for them, and re-layouts  8.15 us (10%)
    pallas_call x1, Pallas kernels, local(): pl.pallas_call(functools.partial(kernel, (NQ, NZ, NY)), out_shape=(jax.Sh...  74.5 us
    unnamed x13, local copies, waits for them, and re-layouts  5.8 us
    pallas_call x1, local copies, waits for them, and re-layouts, local(): pl.pallas_call(functools.partial(kernel, (NQ, NZ, NY)), out_shape=(jax.Sh...  2.35 us

profile of v1, /device:TPU:1, one launch (start us, length us, event | category | flops | bytes accessed | tf_op | source)
XLA Modules:
  0.0 83.3 jit_solution(14324421782147037198)
XLA Ops:
  0.6 2.3 %copy.10.down_h = bf16[1152,288]{1,0:T(8,128)(2,1)} copy(bf16[1152,288]{0,1:T(8,128)(2,1)} %param.8) | data formatting | bytes 1327104 | tf_op args[3]
  2.9 74.5 %shard_map.92 = (f32[8,288]{1,0:T(8,128)}, f32[8,288]{1,0:T(8,128)}, bf16[288,1152]{1,0:T(8,128)(2,1)}, bf16[288,1152]{1,0:T(8,128)(2,1)}, bf16[1152,288]{1,0:T(8,128)(2,1)}) custom-call(bf16[8,288]{1,0:T(8,128)(2,1)} %tok.1, bf16[8,288]{1,0:T(8,128)(2,1)} %cot.1, bf16[288,1152]{1,0:T(8,128)(2,1)} %gate_h.1, bf16[288,1152]{1,0:T(8,128)(2,1)} %up_h.1, ...), custom_call_target="tpu_custom_call" | custom-call | tf_op jit(solution)/shard_map/pallas_call | solution.py:286
  77.5 0.0 copy-start.3
  77.5 0.0 copy-start.1
  77.5 2.4 %copy.11 = bf16[1152,288]{0,1:T(8,128)(2,1)} copy(bf16[1152,288]{1,0:T(8,128)(2,1)} %get-tuple-element.9) | data formatting | bytes 1327104 | tf_op jit(solution)/shard_map/pallas_call | solution.py:286
  79.8 0.0 copy-done.3
  79.9 0.0 copy-start.2
  79.9 0.6 copy.16
  80.5 0.1 copy-done.2
  80.6 0.6 copy.17
  81.2 0.0 copy-done.1
  81.2 0.0 copy-start
  81.2 0.8 %copy.18 = bf16[288,1152]{1,0:T(8,128)(2,1)} copy(bf16[288,1152]{1,0:T(8,128)(2,1)S(1)} %copy-done.1) | data formatting | bytes 1327104
  82.0 0.5 copy-done
  82.5 0.8 %copy.19 = bf16[288,1152]{1,0:T(8,128)(2,1)} copy(bf16[288,1152]{1,0:T(8,128)(2,1)S(1)} %copy-done) | data formatting | bytes 1327104
Async XLA Ops:
  77.5 2.4 %copy-start.3 = (f32[8,288]{1,0:T(8,128)S(1)}, f32[8,288]{1,0:T(8,128)}, u32[]{:S(2)}) copy-start(f32[8,288]{1,0:T(8,128)} %get-tuple-element.15) | copy-start | bytes 27652
  77.5 3.7 %copy-start.1 = (bf16[288,1152]{1,0:T(8,128)(2,1)S(1)}, bf16[288,1152]{1,0:T(8,128)(2,1)}, u32[]{:S(2)}) copy-start(bf16[288,1152]{1,0:T(8,128)(2,1)} %get-tuple-element.17) | copy-start | bytes 1990660
  79.9 0.7 copy-start.2
  81.2 1.3 %copy-start = (bf16[288,1152]{1,0:T(8,128)(2,1)S(1)}, bf16[288,1152]{1,0:T(8,128)(2,1)}, u32[]{:S(2)}) copy-start(bf16[288,1152]{1,0:T(8,128)(2,1)} %get-tuple-element.18) | copy-start | bytes 1990660

commit v2 on v0

v2 whole, which is shorter than its diff:
```python
import functools

import jax
import jax.numpy as jnp
from jax import lax
from jax.experimental import pallas as pl
from jax.experimental.pallas import tpu as pltpu
from jax.sharding import PartitionSpec as P

GELU_SCALE = 0.7978845608028654
CUBIC_TERM = 0.044715
ROWS_DIMS = (((0,), (0,)), ((), ()))
COLS_DIMS = (((1,), (1,)), ((), ()))
MESH_ID = pl.DeviceIdType.MESH
F32 = jnp.float32
BF16 = jnp.bfloat16


def gelu_parts(values):
    tanh_part = jnp.tanh(GELU_SCALE * (values + CUBIC_TERM * values * values * values))
    gelu_value = 0.5 * values * (1.0 + tanh_part)
    gelu_slope = 0.5 * (1.0 + tanh_part) + 0.5 * values * (
        1.0 - tanh_part * tanh_part
    ) * GELU_SCALE * (1.0 + 3.0 * CUBIC_TERM * values * values)
    return (gelu_value, gelu_slope)


def dot(a, b):
    return jnp.dot(a, b, preferred_element_type=F32)


def dot_cols(a, b):
    return lax.dot_general(a, b, COLS_DIMS, preferred_element_type=F32)


def dot_rows(a, b):
    return lax.dot_general(a, b, ROWS_DIMS, preferred_element_type=F32)


def kernel(
    sizes,
    tok, cot, gate_h, up_h, down_h,
    lo_o, gi_o, ggw_o, guw_o, gdw_o,
    GV, UV, DV, WF, DF, WS, DS, XO, XS, TK, CT, PB, RP, HB,
    AZ, RZ, BY, SY, AF, ggw_v, guw_v, gdw_v,
    ld_sem, wx_s, wx_r, py_s, py_r, pz_s, pz_r, xs_s, xs_r, rs_s, rs_r,
    ag_s, ag_r, fw_s, fw_r, a_s, a_r, b_s, b_r, out_sem,
):
    NQ, NZ, NY = sizes
    order = [0] + [k for i in range(1, NZ // 2) for k in (i, NZ - i)] + [NZ // 2]
    slots = NZ // 2
    rows = lo_o.shape[0]
    F, H = DF.shape[1], DF.shape[2]
    part_rows = slots * NY * rows
    R = PB.shape[2]
    dp = lax.axis_index("dp")
    mp = lax.axis_index("mp")
    c = lax.rem(dp, 2)
    oc = 1 - c
    q = lax.div(dp, 2)
    sib = dp + 1 - 2 * c
    z = lax.div(mp, NY)
    y = lax.rem(mp, NY)

    sent = []

    def send(src, dst, ssem, rsem, to_dp, to_mp):
        copy = pltpu.make_async_remote_copy(
            src_ref=src, dst_ref=dst, send_sem=ssem, recv_sem=rsem,
            device_id=(to_dp, to_mp), device_id_type=MESH_ID,
        )
        copy.start()
        sent.append(copy)
        return copy

    def peer(k):
        return 2 * lax.rem(q + k, NQ) + c

    def at_z(k):
        return lax.rem(z + k, NZ) * NY + y

    def at_y(j):
        return z * NY + lax.rem(y + j, NY)

    loads = [
        pltpu.make_async_copy(gate_h, GV, ld_sem.at[0]),
        pltpu.make_async_copy(up_h, UV, ld_sem.at[1]),
        pltpu.make_async_copy(down_h, DV, ld_sem.at[2]),
    ]
    for copy in loads:
        copy.start()

    barrier = pltpu.get_barrier_semaphore()
    partners = [(sib, mp)]
    partners += [(peer(k), mp) for k in range(1, NQ)]
    partners += [(dp, at_z(k)) for k in range(1, NZ)]
    partners += [(dp, at_y(j)) for j in range(1, NY)]
    for partner in partners:
        pl.semaphore_signal(barrier, inc=1, device_id=partner, device_id_type=MESH_ID)
    XO[0, 0] = jnp.concatenate([tok[...].astype(F32), cot[...].astype(F32)], axis=0).astype(BF16)
    pl.semaphore_wait(barrier, len(partners))

    py = [
        send(XO.at[0, 0], XO.at[0, j], py_s.at[j], py_r.at[j], dp, at_y(NY - j))
        for j in range(1, NY)
    ]
    for copy in loads:
        copy.wait()
    for h in range(2):
        half = slice(h * H, (h + 1) * H)
        WF[h] = jnp.concatenate([GV[:, half], UV[:, half]], axis=1)
        DF[h] = DV[:, half]
    wx = [
        send(WF.at[oc], WS, wx_s.at[0], wx_r.at[0], sib, mp),
        send(DF.at[oc], DS, wx_s.at[1], wx_r.at[1], sib, mp),
    ]
    for copy in py:
        copy.wait_recv()
    pz = [None] + [
        send(XO.at[0], XO.at[p], pz_s.at[p], pz_r.at[p], dp, at_z(NZ - order[p]))
        for p in range(1, NZ)
    ]
    xs = [send(XO.at[0], XS.at[0], xs_s.at[0], xs_r.at[0], sib, mp)]

    def rows_of(ref, m):
        both = ref[m * slots : (m + 1) * slots].astype(F32).reshape(slots * NY, 2, rows, F)
        return (
            both[:, 0].reshape(part_rows, F).astype(BF16),
            both[:, 1].reshape(part_rows, F).astype(BF16),
        )

    rs = []
    for m in range(2):
        for p in range(max(1, m * slots), (m + 1) * slots):
            pz[p].wait_recv()
            xs.append(send(XO.at[p], XS.at[p], xs_s.at[p], xs_r.at[p], sib, mp))
        t_own, c_own = rows_of(XO, m)
        TK[m] = t_own
        CT[m] = c_own
        gu = dot(t_own, WF[c])
        gh = dot(c_own, DF[c])
        if m == 0:
            for copy in wx:
                copy.wait_recv()
        for p in range(m * slots, (m + 1) * slots):
            xs[p].wait_recv()
        t_sib, c_sib = rows_of(XS, m)
        gu += dot(t_sib, WS[...])
        PB[m, :, :, 0 : 2 * H] = gu.astype(BF16).reshape(NQ, R, 2 * H)
        gh += dot(c_sib, DS[...])
        PB[m, :, :, 2 * H : 3 * H] = gh.astype(BF16).reshape(NQ, R, H)
        rs.append([
            send(
                PB.at[m, lax.rem(q + k, NQ)], RP.at[m, q], rs_s.at[m, k], rs_r.at[m, k], peer(k), mp
            )
            for k in range(1, NQ)
        ])
        RP[m, q] = PB[m, q]

    ag = []
    fw = []
    for m in range(2):
        for copy in rs[m]:
            copy.wait_recv()
        sums = RP[m, 0].astype(F32)
        for i in range(1, NQ):
            sums += RP[m, i].astype(F32)
        g_sum, u_sum, gh_sum = sums[:, :H], sums[:, H : 2 * H], sums[:, 2 * H :]
        gelu_value, gelu_slope = gelu_parts(g_sum)
        HB[c, m, q] = jnp.concatenate(
            [gh_sum * u_sum * gelu_slope, gh_sum * gelu_value, gelu_value * u_sum], axis=1
        ).astype(BF16)
        block = HB.at[c, m, q]
        ag.append([
            send(block, block, ag_s.at[m, k], ag_r.at[m, k], peer(k), mp) for k in range(1, NQ)
        ])
        fw.append([send(block, block, fw_s.at[m, 0], fw_r.at[m, 0], sib, mp)])

    az = []
    for m in range(2):
        for k in range(1, NQ):
            ag[m][k - 1].wait_recv()
            block = HB.at[c, m, lax.rem(q + NQ - k, NQ)]
            fw[m].append(send(block, block, fw_s.at[m, k], fw_r.at[m, k], sib, mp))
        for copy in fw[m]:
            copy.wait_recv()
        acts = [HB[h, m].reshape(part_rows, 3 * H) for h in range(2)]
        lo = dot_cols(acts[0][:, 2 * H :], DF[0]) + dot_cols(acts[1][:, 2 * H :], DF[1])
        gi = dot_cols(acts[0][:, : 2 * H], WF[0]) + dot_cols(acts[1][:, : 2 * H], WF[1])
        mine = slice(m * slots, (m + 1) * slots)
        AZ[mine, 0] = lo.astype(BF16).reshape(slots, NY * rows, F)
        AZ[mine, 1] = gi.astype(BF16).reshape(slots, NY * rows, F)
        for p in range(max(1, m * slots), (m + 1) * slots):
            az.append(send(AZ.at[p], RZ.at[p], a_s.at[p], a_r.at[p], dp, at_z(order[p])))
        if m == 0:
            RZ[0] = AZ[0]

    tokens_all = TK[...].reshape(2 * part_rows, F)
    cot_all = CT[...].reshape(2 * part_rows, F)

    def full(i):
        halves = [HB[h, :, :, :, i * H : (i + 1) * H].reshape(2 * part_rows, H) for h in range(2)]
        return jnp.concatenate(halves, axis=1)

    AF[...] = full(2)
    gdw_v[...] = dot_rows(cot_all, AF[...]).astype(BF16)
    outs = [pltpu.make_async_copy(gdw_v, gdw_o, out_sem.at[0])]
    outs[0].start()

    for copy in az:
        copy.wait_recv()
    total = RZ[0].astype(F32)
    for p in range(1, NZ):
        total += RZ[p].astype(F32)
    total = total.reshape(2, NY, rows, F)
    for j in range(NY):
        BY[j] = total[:, j]
    by = [
        send(BY.at[j], SY.at[j], b_s.at[j], b_r.at[j], dp, at_y(j)) for j in range(1, NY)
    ]
    SY[0] = BY[0]

    AF[...] = full(0)
    ggw_v[...] = dot_rows(tokens_all, AF[...]).astype(BF16)
    outs.append(pltpu.make_async_copy(ggw_v, ggw_o, out_sem.at[1]))
    outs[1].start()
    AF[...] = full(1)
    guw_v[...] = dot_rows(tokens_all, AF[...]).astype(BF16)
    outs.append(pltpu.make_async_copy(guw_v, guw_o, out_sem.at[2]))
    outs[2].start()

    for copy in by:
        copy.wait_recv()
    last = SY[0]
    for j in range(1, NY):
        last += SY[j]
    lo_o[...] = last[0]
    gi_o[...] = last[1]

    for copy in sent:
        copy.wait_send()
    for copy in outs:
        copy.wait()


def copy_kernel(*refs):
    inward = [pltpu.make_async_copy(refs[i], refs[10 + i], refs[15].at[i]) for i in range(5)]
    outward = [pltpu.make_async_copy(refs[10 + i], refs[5 + i], refs[15].at[5 + i]) for i in range(5)]
    for copy in inward:
        copy.start()
    for i in range(5):
        inward[i].wait()
        outward[i].start()
    for copy in outward:
        copy.wait()


def solution(mesh):
    dp_n, mp_n = mesh.shape["dp"], mesh.shape["mp"]
    NQ, NY = dp_n // 2, min(4, mp_n // 4)
    NZ = mp_n // NY

    def local(tokens, gate_weight, up_weight, down_weight, cotangent):
        rows, F = tokens.shape
        U = gate_weight.shape[1]
        H = U // 2
        T = rows * mp_n
        R = T // dp_n
        dma = pltpu.SemaphoreType.DMA
        vmem = pl.BlockSpec(memory_space=pltpu.VMEM)
        hbm = pl.BlockSpec(memory_space=pl.ANY)
        limit = pltpu.CompilerParams(vmem_limit_bytes=60 * 1024 * 1024)
        scratch = [
            ((F, U), BF16), ((F, U), BF16), ((F, U), BF16),
            ((2, F, U), BF16), ((2, F, H), BF16), ((F, U), BF16), ((F, H), BF16),
            ((NZ, NY, 2 * rows, F), BF16), ((NZ, NY, 2 * rows, F), BF16),
            ((2, T // 2, F), BF16), ((2, T // 2, F), BF16),
            ((2, NQ, R, 3 * H), BF16), ((2, NQ, R, 3 * H), BF16), ((2, 2, NQ, R, 3 * H), BF16),
            ((NZ, 2, NY * rows, F), BF16), ((NZ, 2, NY * rows, F), BF16),
            ((NY, 2, rows, F), F32), ((NY, 2, rows, F), F32), ((T, U), BF16),
            ((F, U), BF16), ((F, U), BF16), ((F, U), BF16),
        ]
        sems = [(3,), (2,), (2,), (NY,), (NY,), (NZ,), (NZ,), (NZ,), (NZ,), (2, NQ), (2, NQ),
                (2, NQ), (2, NQ), (2, NQ), (2, NQ), (NZ,), (NZ,), (NY,), (NY,), (3,)]
        shapes = (
            jax.ShapeDtypeStruct((rows, F), F32), jax.ShapeDtypeStruct((rows, F), F32),
            jax.ShapeDtypeStruct((F, U), BF16), jax.ShapeDtypeStruct((F, U), BF16),
            jax.ShapeDtypeStruct((F, U), BF16),
        )
        results = pl.pallas_call(
            functools.partial(kernel, (NQ, NZ, NY)),
            out_shape=shapes,
            in_specs=[vmem, vmem, hbm, hbm, hbm],
            out_specs=(vmem, vmem, hbm, hbm, hbm),
            scratch_shapes=[pltpu.VMEM(s, t) for s, t in scratch] + [dma(n) for n in sems],
            compiler_params=pltpu.CompilerParams(
                collective_id=0, has_side_effects=True, vmem_limit_bytes=56 * 1024 * 1024
            ),
        )(tokens, cotangent, gate_weight, up_weight, down_weight.T)
        lo, gi, ggw, guw, gdw = pl.pallas_call(
            copy_kernel,
            out_shape=shapes,
            in_specs=[hbm] * 5,
            out_specs=(hbm,) * 5,
            scratch_shapes=[pltpu.VMEM(x.shape, x.dtype) for x in shapes] + [dma((10,))],
            compiler_params=limit,
        )(*results)
        return lo, gi, ggw, guw, gdw.T

    return jax.shard_map(
        local,
        mesh=mesh,
        in_specs=(P("mp", "dp"), P("dp", "mp"), P("dp", "mp"), P("mp", "dp"), P("mp", "dp")),
        out_specs=(P("mp", "dp"), P("mp", "dp"), P("dp", "mp"), P("dp", "mp"), P("mp", "dp")),
        check_vma=False,
    )
```

time: 631 us -> 72.6 us (0.12)
  the two profiles are of different devices: /device:TPU:2 before, /device:TPU:72 now
where the time goes in v2:
time: 72.6 us; the launch traced here: 72.3 us
  Pallas kernels  71.7 us (99%)
    pallas_call x1, Pallas kernels, local(): pl.pallas_call(functools.partial(kernel, (NQ, NZ, NY)), out_shape=shapes,...  69.2 us
    pallas_call x1, Pallas kernels, local(): pl.pallas_call(copy_kernel, out_shape=shapes, in_specs=[hbm] * 5, out_spe...  2.49 us

profile of v2, /device:TPU:72, one launch (start us, length us, event | category | flops | bytes accessed | tf_op | source)
XLA Modules:
  0.0 72.3 jit_solution(12061759724416863893)
XLA Ops:
  0.6 69.2 %shard_map.92 = (f32[8,288]{1,0:T(8,128)}, f32[8,288]{1,0:T(8,128)}, bf16[288,1152]{1,0:T(8,128)(2,1)}, bf16[288,1152]{1,0:T(8,128)(2,1)}, bf16[288,1152]{1,0:T(8,128)(2,1)}) custom-call(bf16[8,288]{1,0:T(8,128)(2,1)} %tok.1, bf16[8,288]{1,0:T(8,128)(2,1)} %cot.1, bf16[288,1152]{1,0:T(8,128)(2,1)} %gate_h.1, bf16[288,1152]{1,0:T(8,128)(2,1)} %up_h.1, ...), custom_call_target="tpu_custom_call" | custom-call | tf_op jit(solution)/shard_map/pallas_call | solution.py:290
  69.8 2.5 %shard_map.93 = (f32[8,288]{1,0:T(8,128)}, f32[8,288]{1,0:T(8,128)}, bf16[288,1152]{1,0:T(8,128)(2,1)}, bf16[288,1152]{1,0:T(8,128)(2,1)}, bf16[288,1152]{1,0:T(8,128)(2,1)}) custom-call(f32[8,288]{1,0:T(8,128)} %get-tuple-element.15.refs_0_, f32[8,288]{1,0:T(8,128)} %get-tuple-element.16.refs_1_, bf16[288,1152]{1,0:T(8,128)(2,1)} %get-tuple-element.17.refs_2_, ...), custom_call_target="tpu_custom_call" | custom-call | tf_op jit(solution)/shard_map/pallas_call | solution.py:300

commit v3 on v2

--- a/solution.py
+++ b/solution.py
@@ -39,12 +39,12 @@
 
 def kernel(
     sizes,
-    tok, cot, gate_h, up_h, down_h,
+    tok_h, cot_h, gate_h, up_h, down_h,
     lo_o, gi_o, ggw_o, guw_o, gdw_o,
-    GV, UV, DV, WF, DF, WS, DS, XO, XS, TK, CT, PB, RP, HB,
-    AZ, RZ, BY, SY, AF, ggw_v, guw_v, gdw_v,
+    tok, cot, GV, UV, DV, WF, DF, WS, DS, XO, XS, TK, CT, PB, RP, HB,
+    AY, RY, AZ, RZ, BY, SY, BZ, SZ, AF, ggw_v, guw_v, gdw_v,
     ld_sem, wx_s, wx_r, py_s, py_r, pz_s, pz_r, xs_s, xs_r, rs_s, rs_r,
-    ag_s, ag_r, fw_s, fw_r, a_s, a_r, b_s, b_r, out_sem,
+    ag_s, ag_r, fw_s, fw_r, ay_s, ay_r, az_s, az_r, by_s, by_r, bz_s, bz_r, out_sem,
 ):
     NQ, NZ, NY = sizes
     order = [0] + [k for i in range(1, NZ // 2) for k in (i, NZ - i)] + [NZ // 2]
@@ -73,8 +73,22 @@
         sent.append(copy)
         return copy
 
+    NX = NQ // 2
+    qx = lax.div(q, 2)
+    qy = lax.rem(q, 2)
+    steps = [(dx, dy) for dx in range(NX) for dy in range(2)][1:]
+    steps.sort(key=lambda s: -min(s[0], NX - s[0]) - s[1])
+
+    def ahead(k):
+        dx, dy = steps[k - 1]
+        return 2 * lax.rem(qx + dx, NX) + lax.rem(qy + dy, 2)
+
+    def behind(k):
+        dx, dy = steps[k - 1]
+        return 2 * lax.rem(qx + NX - dx, NX) + lax.rem(qy + dy, 2)
+
     def peer(k):
-        return 2 * lax.rem(q + k, NQ) + c
+        return 2 * ahead(k) + c
 
     def at_z(k):
         return lax.rem(z + k, NZ) * NY + y
@@ -87,6 +101,12 @@
         pltpu.make_async_copy(up_h, UV, ld_sem.at[1]),
         pltpu.make_async_copy(down_h, DV, ld_sem.at[2]),
     ]
+    rows_in = [
+        pltpu.make_async_copy(tok_h, tok, ld_sem.at[3]),
+        pltpu.make_async_copy(cot_h, cot, ld_sem.at[4]),
+    ]
+    for copy in rows_in:
+        copy.start()
     for copy in loads:
         copy.start()
 
@@ -97,6 +117,8 @@
     partners += [(dp, at_y(j)) for j in range(1, NY)]
     for partner in partners:
         pl.semaphore_signal(barrier, inc=1, device_id=partner, device_id_type=MESH_ID)
+    for copy in rows_in:
+        copy.wait()
     XO[0, 0] = jnp.concatenate([tok[...].astype(F32), cot[...].astype(F32)], axis=0).astype(BF16)
     pl.semaphore_wait(barrier, len(partners))
 
@@ -151,7 +173,7 @@
         PB[m, :, :, 2 * H : 3 * H] = gh.astype(BF16).reshape(NQ, R, H)
         rs.append([
             send(
-                PB.at[m, lax.rem(q + k, NQ)], RP.at[m, q], rs_s.at[m, k], rs_r.at[m, k], peer(k), mp
+                PB.at[m, ahead(k)], RP.at[m, q], rs_s.at[m, k], rs_r.at[m, k], peer(k), mp
             )
             for k in range(1, NQ)
         ])
@@ -177,21 +199,29 @@
         fw.append([send(block, block, fw_s.at[m, 0], fw_r.at[m, 0], sib, mp)])
 
     az = []
+    ay = []
     for m in range(2):
         for k in range(1, NQ):
             ag[m][k - 1].wait_recv()
-            block = HB.at[c, m, lax.rem(q + NQ - k, NQ)]
+            block = HB.at[c, m, behind(k)]
             fw[m].append(send(block, block, fw_s.at[m, k], fw_r.at[m, k], sib, mp))
+        acts = HB[c, m].reshape(part_rows, 3 * H)
+        lo = dot_cols(acts[:, 2 * H :], DF[c])
+        gi = dot_cols(acts[:, : 2 * H], WF[c])
         for copy in fw[m]:
             copy.wait_recv()
-        acts = [HB[h, m].reshape(part_rows, 3 * H) for h in range(2)]
-        lo = dot_cols(acts[0][:, 2 * H :], DF[0]) + dot_cols(acts[1][:, 2 * H :], DF[1])
-        gi = dot_cols(acts[0][:, : 2 * H], WF[0]) + dot_cols(acts[1][:, : 2 * H], WF[1])
-        mine = slice(m * slots, (m + 1) * slots)
-        AZ[mine, 0] = lo.astype(BF16).reshape(slots, NY * rows, F)
-        AZ[mine, 1] = gi.astype(BF16).reshape(slots, NY * rows, F)
+        acts = HB[oc, m].reshape(part_rows, 3 * H)
+        lo += dot_cols(acts[:, 2 * H :], DF[oc])
+        lo = lo.reshape(slots, NY, rows, F)
+        for j in range(NY):
+            AY[m, j] = lo[:, j].reshape(slots * rows, F).astype(BF16)
+        for j in range(1, NY):
+            ay.append(send(AY.at[m, j], RY.at[m, j], ay_s.at[m, j], ay_r.at[m, j], dp, at_y(j)))
+        RY[m, 0] = AY[m, 0]
+        gi += dot_cols(acts[:, : 2 * H], WF[oc])
+        AZ[m * slots : (m + 1) * slots] = gi.astype(BF16).reshape(slots, NY * rows, F)
         for p in range(max(1, m * slots), (m + 1) * slots):
-            az.append(send(AZ.at[p], RZ.at[p], a_s.at[p], a_r.at[p], dp, at_z(order[p])))
+            az.append(send(AZ.at[p], RZ.at[p], az_s.at[p], az_r.at[p], dp, at_z(order[p])))
         if m == 0:
             RZ[0] = AZ[0]
 
@@ -207,18 +237,24 @@
     outs = [pltpu.make_async_copy(gdw_v, gdw_o, out_sem.at[0])]
     outs[0].start()
 
+    for copy in ay:
+        copy.wait_recv()
+    total = RY[:, 0].astype(F32)
+    for j in range(1, NY):
+        total += RY[:, j].astype(F32)
+    BZ[...] = total.reshape(NZ, rows, F)
+    bz = [
+        send(BZ.at[p], SZ.at[p], bz_s.at[p], bz_r.at[p], dp, at_z(order[p])) for p in range(1, NZ)
+    ]
     for copy in az:
         copy.wait_recv()
     total = RZ[0].astype(F32)
     for p in range(1, NZ):
         total += RZ[p].astype(F32)
-    total = total.reshape(2, NY, rows, F)
-    for j in range(NY):
-        BY[j] = total[:, j]
+    BY[...] = total.reshape(NY, rows, F)
     by = [
-        send(BY.at[j], SY.at[j], b_s.at[j], b_r.at[j], dp, at_y(j)) for j in range(1, NY)
-    ]
-    SY[0] = BY[0]
+        send(BY.at[j], SY.at[j], by_s.at[j], by_r.at[j], dp, at_y(j)) for j in range(1, NY)
+    ]
 
     AF[...] = full(0)
     ggw_v[...] = dot_rows(tokens_all, AF[...]).astype(BF16)
@@ -231,11 +267,16 @@
 
     for copy in by:
         copy.wait_recv()
-    last = SY[0]
+    last = BY[0]
     for j in range(1, NY):
         last += SY[j]
-    lo_o[...] = last[0]
-    gi_o[...] = last[1]
+    gi_o[...] = last
+    for copy in bz:
+        copy.wait_recv()
+    last = BZ[0]
+    for p in range(1, NZ):
+        last += SZ[p]
+    lo_o[...] = last
 
     for copy in sent:
         copy.wait_send()
@@ -244,13 +285,13 @@
 
 
 def copy_kernel(*refs):
-    inward = [pltpu.make_async_copy(refs[i], refs[10 + i], refs[15].at[i]) for i in range(5)]
-    outward = [pltpu.make_async_copy(refs[10 + i], refs[5 + i], refs[15].at[5 + i]) for i in range(5)]
+    inward = [pltpu.make_async_copy(refs[i], refs[10 + i], refs[15].at[0, i]) for i in range(5)]
+    outward = [pltpu.make_async_copy(refs[10 + i], refs[5 + i], refs[15].at[1, i]) for i in range(5)]
     for copy in inward:
         copy.start()
-    for i in range(5):
-        inward[i].wait()
-        outward[i].start()
+    for come, go in zip(inward, outward):
+        come.wait()
+        go.start()
     for copy in outward:
         copy.wait()
 
@@ -268,20 +309,25 @@
         R = T // dp_n
         dma = pltpu.SemaphoreType.DMA
         vmem = pl.BlockSpec(memory_space=pltpu.VMEM)
-        hbm = pl.BlockSpec(memory_space=pl.ANY)
+        hbm = pl.BlockSpec(memory_space=pltpu.HBM)
+        anywhere = pl.BlockSpec(memory_space=pl.ANY)
         limit = pltpu.CompilerParams(vmem_limit_bytes=60 * 1024 * 1024)
         scratch = [
+            ((rows, F), BF16), ((rows, F), BF16),
             ((F, U), BF16), ((F, U), BF16), ((F, U), BF16),
             ((2, F, U), BF16), ((2, F, H), BF16), ((F, U), BF16), ((F, H), BF16),
             ((NZ, NY, 2 * rows, F), BF16), ((NZ, NY, 2 * rows, F), BF16),
             ((2, T // 2, F), BF16), ((2, T // 2, F), BF16),
             ((2, NQ, R, 3 * H), BF16), ((2, NQ, R, 3 * H), BF16), ((2, 2, NQ, R, 3 * H), BF16),
-            ((NZ, 2, NY * rows, F), BF16), ((NZ, 2, NY * rows, F), BF16),
-            ((NY, 2, rows, F), F32), ((NY, 2, rows, F), F32), ((T, U), BF16),
+            ((2, NY, NZ // 2 * rows, F), BF16), ((2, NY, NZ // 2 * rows, F), BF16),
+            ((NZ, NY * rows, F), BF16), ((NZ, NY * rows, F), BF16),
+            ((NY, rows, F), F32), ((NY, rows, F), F32),
+            ((NZ, rows, F), F32), ((NZ, rows, F), F32), ((T, U), BF16),
             ((F, U), BF16), ((F, U), BF16), ((F, U), BF16),
         ]
-        sems = [(3,), (2,), (2,), (NY,), (NY,), (NZ,), (NZ,), (NZ,), (NZ,), (2, NQ), (2, NQ),
-                (2, NQ), (2, NQ), (2, NQ), (2, NQ), (NZ,), (NZ,), (NY,), (NY,), (3,)]
+        sems = [(5,), (2,), (2,), (NY,), (NY,), (NZ,), (NZ,), (NZ,), (NZ,), (2, NQ), (2, NQ),
+                (2, NQ), (2, NQ), (2, NQ), (2, NQ), (2, NY), (2, NY), (NZ,), (NZ,),
+                (NY,), (NY,), (NZ,), (NZ,), (3,)]
         shapes = (
             jax.ShapeDtypeStruct((rows, F), F32), jax.ShapeDtypeStruct((rows, F), F32),
             jax.ShapeDtypeStruct((F, U), BF16), jax.ShapeDtypeStruct((F, U), BF16),
@@ -290,8 +336,8 @@
         results = pl.pallas_call(
             functools.partial(kernel, (NQ, NZ, NY)),
             out_shape=shapes,
-            in_specs=[vmem, vmem, hbm, hbm, hbm],
-            out_specs=(vmem, vmem, hbm, hbm, hbm),
+            in_specs=[hbm] * 5,
+            out_specs=(vmem, vmem, anywhere, anywhere, anywhere),
             scratch_shapes=[pltpu.VMEM(s, t) for s, t in scratch] + [dma(n) for n in sems],
             compiler_params=pltpu.CompilerParams(
                 collective_id=0, has_side_effects=True, vmem_limit_bytes=56 * 1024 * 1024
@@ -300,9 +346,9 @@
         lo, gi, ggw, guw, gdw = pl.pallas_call(
             copy_kernel,
             out_shape=shapes,
-            in_specs=[hbm] * 5,
-            out_specs=(hbm,) * 5,
-            scratch_shapes=[pltpu.VMEM(x.shape, x.dtype) for x in shapes] + [dma((10,))],
+            in_specs=[anywhere] * 5,
+            out_specs=(anywhere,) * 5,
+            scratch_shapes=[pltpu.VMEM(x.shape, x.dtype) for x in shapes] + [dma((2, 5))],
             compiler_params=limit,
         )(*results)
         return lo, gi, ggw, guw, gdw.T

time: 72.6 us -> 69.4 us (0.956)
  the two profiles are of different devices: /device:TPU:72 before, /device:TPU:1 now
where the time goes in v3:
time: 69.4 us; the launch traced here: 69.2 us
  Pallas kernels  68.5 us (99%)
    pallas_call x1, Pallas kernels, local(): pl.pallas_call(functools.partial(kernel, (NQ, NZ, NY)), out_shape=shapes,...  66 us
    pallas_call x1, Pallas kernels, local(): pl.pallas_call(copy_kernel, out_shape=shapes, in_specs=[anywhere] * 5, ou...  2.49 us

profile of v3, /device:TPU:1, one launch (start us, length us, event | category | flops | bytes accessed | tf_op | source)
XLA Modules:
  0.0 69.2 jit_solution(3166842885968794338)
XLA Ops:
  0.6 66.0 %shard_map.92 = (f32[8,288]{1,0:T(8,128)}, f32[8,288]{1,0:T(8,128)}, bf16[288,1152]{1,0:T(8,128)(2,1)}, bf16[288,1152]{1,0:T(8,128)(2,1)}, bf16[288,1152]{1,0:T(8,128)(2,1)}) custom-call(bf16[8,288]{1,0:T(8,128)(2,1)} %tok_h.1, bf16[8,288]{1,0:T(8,128)(2,1)} %cot_h.1, bf16[288,1152]{1,0:T(8,128)(2,1)} %gate_h.1, bf16[288,1152]{1,0:T(8,128)(2,1)} %up_h.1, ...), custom_call_target="tpu_custom_call" | custom-call | tf_op jit(solution)/shard_map/pallas_call | solution.py:336
  66.7 2.5 %shard_map.93 = (f32[8,288]{1,0:T(8,128)}, f32[8,288]{1,0:T(8,128)}, bf16[288,1152]{1,0:T(8,128)(2,1)}, bf16[288,1152]{1,0:T(8,128)(2,1)}, bf16[288,1152]{1,0:T(8,128)(2,1)}) custom-call(f32[8,288]{1,0:T(8,128)} %get-tuple-element.15.refs_0_, f32[8,288]{1,0:T(8,128)} %get-tuple-element.16.refs_1_, bf16[288,1152]{1,0:T(8,128)(2,1)} %get-tuple-element.17.refs_2_, ...), custom_call_target="tpu_custom_call" | custom-call | tf_op jit(solution)/shard_map/pallas_call | solution.py:346

commit v4 on v3

--- a/solution.py
+++ b/solution.py
@@ -14,6 +14,7 @@
 MESH_ID = pl.DeviceIdType.MESH
 F32 = jnp.float32
 BF16 = jnp.bfloat16
+LANES = 128
 
 
 def gelu_parts(values):
@@ -41,13 +42,15 @@
     sizes,
     tok_h, cot_h, gate_h, up_h, down_h,
     lo_o, gi_o, ggw_o, guw_o, gdw_o,
-    tok, cot, GV, UV, DV, WF, DF, WS, DS, XO, XS, TK, CT, PB, RP, HB,
+    tok, cot, GV, UV, DV, WF, DF, WS, DS, XY, XO, XS, TK, CT, PB, RP, HB,
     AY, RY, AZ, RZ, BY, SY, BZ, SZ, AF, ggw_v, guw_v, gdw_v,
     ld_sem, wx_s, wx_r, py_s, py_r, pz_s, pz_r, xs_s, xs_r, rs_s, rs_r,
     ag_s, ag_r, fw_s, fw_r, ay_s, ay_r, az_s, az_r, by_s, by_r, bz_s, bz_r, out_sem,
 ):
     NQ, NZ, NY = sizes
-    order = [0] + [k for i in range(1, NZ // 2) for k in (i, NZ - i)] + [NZ // 2]
+    order = [0]
+    for first in (2, 1):
+        order += sorted(range(first, NZ, 2), key=lambda k: -min(k, NZ - k))
     slots = NZ // 2
     rows = lo_o.shape[0]
     F, H = DF.shape[1], DF.shape[2]
@@ -119,12 +122,12 @@
         pl.semaphore_signal(barrier, inc=1, device_id=partner, device_id_type=MESH_ID)
     for copy in rows_in:
         copy.wait()
-    XO[0, 0] = jnp.concatenate([tok[...].astype(F32), cot[...].astype(F32)], axis=0).astype(BF16)
+    XY[0] = jnp.concatenate([tok[...].astype(F32), cot[...].astype(F32)], axis=0).astype(BF16)
     pl.semaphore_wait(barrier, len(partners))
 
     py = [
-        send(XO.at[0, 0], XO.at[0, j], py_s.at[j], py_r.at[j], dp, at_y(NY - j))
-        for j in range(1, NY)
+        send(XY.at[0], XY.at[j], py_s.at[j], py_r.at[j], dp, at_y(NY - j))
+        for j in sorted(range(1, NY), key=lambda j: -min(j, NY - j))
     ]
     for copy in loads:
         copy.wait()
@@ -138,6 +141,17 @@
     ]
     for copy in py:
         copy.wait_recv()
+    lanes = XO.shape[2]
+    whole, rest = F // lanes, F % lanes
+    block_rows = NY * 2 * rows
+    for t in range(whole):
+        XO[0, t * block_rows : (t + 1) * block_rows] = XY[
+            :, :, t * lanes : (t + 1) * lanes
+        ].reshape(block_rows, lanes)
+    if rest:
+        XO[0, whole * block_rows :] = jnp.concatenate(
+            [XY[j, :, whole * lanes :] for j in range(NY)], axis=1
+        )
     pz = [None] + [
         send(XO.at[0], XO.at[p], pz_s.at[p], pz_r.at[p], dp, at_z(NZ - order[p]))
         for p in range(1, NZ)
@@ -145,7 +159,13 @@
     xs = [send(XO.at[0], XS.at[0], xs_s.at[0], xs_r.at[0], sib, mp)]
 
     def rows_of(ref, m):
-        both = ref[m * slots : (m + 1) * slots].astype(F32).reshape(slots * NY, 2, rows, F)
+        packed = ref[m * slots : (m + 1) * slots].astype(F32)
+        both = [packed[:, t * block_rows : (t + 1) * block_rows] for t in range(whole)]
+        if rest:
+            last = packed[:, whole * block_rows :]
+            last = [last[:, :, j * rest : (j + 1) * rest] for j in range(NY)]
+            both.append(jnp.stack(last, axis=1).reshape(slots, block_rows, rest))
+        both = jnp.concatenate(both, axis=2).reshape(slots * NY, 2, rows, F)
         return (
             both[:, 0].reshape(part_rows, F).astype(BF16),
             both[:, 1].reshape(part_rows, F).astype(BF16),
@@ -201,7 +221,7 @@
     az = []
     ay = []
     for m in range(2):
-        for k in range(1, NQ):
+        for k in range(NQ - 1, 0, -1):
             ag[m][k - 1].wait_recv()
             block = HB.at[c, m, behind(k)]
             fw[m].append(send(block, block, fw_s.at[m, k], fw_r.at[m, k], sib, mp))
@@ -305,6 +325,7 @@
         rows, F = tokens.shape
         U = gate_weight.shape[1]
         H = U // 2
+        packed = F // LANES * NY * 2 * rows + (2 * rows if F % LANES else 0)
         T = rows * mp_n
         R = T // dp_n
         dma = pltpu.SemaphoreType.DMA
@@ -316,7 +337,7 @@
             ((rows, F), BF16), ((rows, F), BF16),
             ((F, U), BF16), ((F, U), BF16), ((F, U), BF16),
             ((2, F, U), BF16), ((2, F, H), BF16), ((F, U), BF16), ((F, H), BF16),
-            ((NZ, NY, 2 * rows, F), BF16), ((NZ, NY, 2 * rows, F), BF16),
+            ((NY, 2 * rows, F), BF16), ((NZ, packed, LANES), BF16), ((NZ, packed, LANES), BF16),
             ((2, T // 2, F), BF16), ((2, T // 2, F), BF16),
             ((2, NQ, R, 3 * H), BF16), ((2, NQ, R, 3 * H), BF16), ((2, 2, NQ, R, 3 * H), BF16),
             ((2, NY, NZ // 2 * rows, F), BF16), ((2, NY, NZ // 2 * rows, F), BF16),

time: 69.4 us -> 68.5 us (0.987)
  Pallas kernels: 68.5 us -> 67.6 us
    pallas_call x1, Pallas kernels: 66 us -> 65.1 us  [local(): pl.pallas_call(functools.partial(kernel, (NQ, NZ, NY)), out_shape=shapes,...]
where the time goes in v4:
time: 68.5 us; the launch traced here: 68.2 us
  Pallas kernels  67.6 us (99%)
    pallas_call x1, Pallas kernels, local(): pl.pallas_call(functools.partial(kernel, (NQ, NZ, NY)), out_shape=shapes,...  65.1 us
    pallas_call x1, Pallas kernels, local(): pl.pallas_call(copy_kernel, out_shape=shapes, in_specs=[anywhere] * 5, ou...  2.49 us

profile of v4, /device:TPU:1, one launch (start us, length us, event | category | flops | bytes accessed | tf_op | source)
XLA Modules:
  0.0 68.2 jit_solution(2240880929695133049)
XLA Ops:
  0.6 65.1 %shard_map.92 = (f32[8,288]{1,0:T(8,128)}, f32[8,288]{1,0:T(8,128)}, bf16[288,1152]{1,0:T(8,128)(2,1)}, bf16[288,1152]{1,0:T(8,128)(2,1)}, bf16[288,1152]{1,0:T(8,128)(2,1)}) custom-call(bf16[8,288]{1,0:T(8,128)(2,1)} %tok_h.1, bf16[8,288]{1,0:T(8,128)(2,1)} %cot_h.1, bf16[288,1152]{1,0:T(8,128)(2,1)} %gate_h.1, bf16[288,1152]{1,0:T(8,128)(2,1)} %up_h.1, ...), custom_call_target="tpu_custom_call" | custom-call | tf_op jit(solution)/shard_map/pallas_call | solution.py:357
  65.7 2.5 %shard_map.93 = (f32[8,288]{1,0:T(8,128)}, f32[8,288]{1,0:T(8,128)}, bf16[288,1152]{1,0:T(8,128)(2,1)}, bf16[288,1152]{1,0:T(8,128)(2,1)}, bf16[288,1152]{1,0:T(8,128)(2,1)}) custom-call(f32[8,288]{1,0:T(8,128)} %get-tuple-element.15.refs_0_, f32[8,288]{1,0:T(8,128)} %get-tuple-element.16.refs_1_, bf16[288,1152]{1,0:T(8,128)(2,1)} %get-tuple-element.17.refs_2_, ...), custom_call_target="tpu_custom_call" | custom-call | tf_op jit(solution)/shard_map/pallas_call | solution.py:367

commit v5 on v4

--- a/solution.py
+++ b/solution.py
@@ -41,9 +41,9 @@
 def kernel(
     sizes,
     tok_h, cot_h, gate_h, up_h, down_h,
-    lo_o, gi_o, ggw_o, guw_o, gdw_o,
+    SZ, SY, ggw_o, guw_o, gdw_o,
     tok, cot, GV, UV, DV, WF, DF, WS, DS, XY, XO, XS, TK, CT, PB, RP, HB,
-    AY, RY, AZ, RZ, BY, SY, BZ, SZ, AF, ggw_v, guw_v, gdw_v,
+    AY, RY, AZ, RZ, BY, BZ, AF, ggw_v, guw_v, gdw_v,
     ld_sem, wx_s, wx_r, py_s, py_r, pz_s, pz_r, xs_s, xs_r, rs_s, rs_r,
     ag_s, ag_r, fw_s, fw_r, ay_s, ay_r, az_s, az_r, by_s, by_r, bz_s, bz_r, out_sem,
 ):
@@ -52,7 +52,7 @@
     for first in (2, 1):
         order += sorted(range(first, NZ, 2), key=lambda k: -min(k, NZ - k))
     slots = NZ // 2
-    rows = lo_o.shape[0]
+    rows = tok.shape[0]
     F, H = DF.shape[1], DF.shape[2]
     part_rows = slots * NY * rows
     R = PB.shape[2]
@@ -75,6 +75,11 @@
         copy.start()
         sent.append(copy)
         return copy
+
+    def drain(n):
+        for copy in sent[:n]:
+            copy.wait_send()
+        del sent[:n]
 
     NX = NQ // 2
     qx = lax.div(q, 2)
@@ -285,33 +290,37 @@
     outs.append(pltpu.make_async_copy(guw_v, guw_o, out_sem.at[2]))
     outs[2].start()
 
-    for copy in by:
+    outs.append(pltpu.make_async_copy(BZ.at[0], SZ.at[0], out_sem.at[3]))
+    outs[3].start()
+    outs.append(pltpu.make_async_copy(BY.at[0], SY.at[0], out_sem.at[4]))
+    outs[4].start()
+    drain(len(sent) - len(by) - len(bz))
+    for copy in outs[:2]:
+        copy.wait()
+    for copy in by + bz:
         copy.wait_recv()
-    last = BY[0]
-    for j in range(1, NY):
-        last += SY[j]
-    gi_o[...] = last
-    for copy in bz:
-        copy.wait_recv()
-    last = BZ[0]
-    for p in range(1, NZ):
-        last += SZ[p]
-    lo_o[...] = last
-
-    for copy in sent:
-        copy.wait_send()
-    for copy in outs:
-        copy.wait()
-
-
-def copy_kernel(*refs):
-    inward = [pltpu.make_async_copy(refs[i], refs[10 + i], refs[15].at[0, i]) for i in range(5)]
-    outward = [pltpu.make_async_copy(refs[10 + i], refs[5 + i], refs[15].at[1, i]) for i in range(5)]
+    drain(len(sent))
+    for copy in outs[2:]:
+        copy.wait()
+
+
+def closing_kernel(*refs):
+    came, sem = refs[10:15], refs[17]
+    gone = refs[15:17] + refs[12:15]
+    inward = [pltpu.make_async_copy(refs[i], came[i], sem.at[0, i]) for i in range(5)]
+    outward = [pltpu.make_async_copy(gone[i], refs[5 + i], sem.at[1, i]) for i in range(5)]
     for copy in inward:
         copy.start()
-    for come, go in zip(inward, outward):
-        come.wait()
-        go.start()
+    for i in range(2):
+        inward[i].wait()
+        last = came[i][0]
+        for j in range(1, came[i].shape[0]):
+            last += came[i][j]
+        gone[i][...] = last
+        outward[i].start()
+    for i in range(2, 5):
+        inward[i].wait()
+        outward[i].start()
     for copy in outward:
         copy.wait()
 
@@ -329,7 +338,6 @@
         T = rows * mp_n
         R = T // dp_n
         dma = pltpu.SemaphoreType.DMA
-        vmem = pl.BlockSpec(memory_space=pltpu.VMEM)
         hbm = pl.BlockSpec(memory_space=pltpu.HBM)
         anywhere = pl.BlockSpec(memory_space=pl.ANY)
         limit = pltpu.CompilerParams(vmem_limit_bytes=60 * 1024 * 1024)
@@ -342,34 +350,37 @@
             ((2, NQ, R, 3 * H), BF16), ((2, NQ, R, 3 * H), BF16), ((2, 2, NQ, R, 3 * H), BF16),
             ((2, NY, NZ // 2 * rows, F), BF16), ((2, NY, NZ // 2 * rows, F), BF16),
             ((NZ, NY * rows, F), BF16), ((NZ, NY * rows, F), BF16),
-            ((NY, rows, F), F32), ((NY, rows, F), F32),
-            ((NZ, rows, F), F32), ((NZ, rows, F), F32), ((T, U), BF16),
+            ((NY, rows, F), F32), ((NZ, rows, F), F32), ((T, U), BF16),
             ((F, U), BF16), ((F, U), BF16), ((F, U), BF16),
         ]
         sems = [(5,), (2,), (2,), (NY,), (NY,), (NZ,), (NZ,), (NZ,), (NZ,), (2, NQ), (2, NQ),
                 (2, NQ), (2, NQ), (2, NQ), (2, NQ), (2, NY), (2, NY), (NZ,), (NZ,),
-                (NY,), (NY,), (NZ,), (NZ,), (3,)]
+                (NY,), (NY,), (NZ,), (NZ,), (5,)]
         shapes = (
             jax.ShapeDtypeStruct((rows, F), F32), jax.ShapeDtypeStruct((rows, F), F32),
             jax.ShapeDtypeStruct((F, U), BF16), jax.ShapeDtypeStruct((F, U), BF16),
             jax.ShapeDtypeStruct((F, U), BF16),
         )
+        terms = (
+            jax.ShapeDtypeStruct((NZ, rows, F), F32), jax.ShapeDtypeStruct((NY, rows, F), F32),
+        )
         results = pl.pallas_call(
             functools.partial(kernel, (NQ, NZ, NY)),
-            out_shape=shapes,
+            out_shape=terms + shapes[2:],
             in_specs=[hbm] * 5,
-            out_specs=(vmem, vmem, anywhere, anywhere, anywhere),
+            out_specs=(anywhere,) * 5,
             scratch_shapes=[pltpu.VMEM(s, t) for s, t in scratch] + [dma(n) for n in sems],
             compiler_params=pltpu.CompilerParams(
                 collective_id=0, has_side_effects=True, vmem_limit_bytes=56 * 1024 * 1024
             ),
         )(tokens, cotangent, gate_weight, up_weight, down_weight.T)
         lo, gi, ggw, guw, gdw = pl.pallas_call(
-            copy_kernel,
+            closing_kernel,
             out_shape=shapes,
             in_specs=[anywhere] * 5,
             out_specs=(anywhere,) * 5,
-            scratch_shapes=[pltpu.VMEM(x.shape, x.dtype) for x in shapes] + [dma((2, 5))],
+            scratch_shapes=[pltpu.VMEM(x.shape, x.dtype) for x in terms + shapes[2:] + shapes[:2]]
+            + [dma((2, 5))],
             compiler_params=limit,
         )(*results)
         return lo, gi, ggw, guw, gdw.T

time: 68.5 us -> 67.8 us (0.990)
  no operation moved by 1% of the time
where the time goes in v5:
time: 67.8 us; the launch traced here: 67.6 us
  Pallas kernels  67 us (99%)
    pallas_call x1, Pallas kernels, local(): pl.pallas_call(functools.partial(kernel, (NQ, NZ, NY)), out_shape=terms +...  64.4 us
    pallas_call x1, Pallas kernels, local(): pl.pallas_call(closing_kernel, out_shape=shapes, in_specs=[anywhere] * 5,...  2.54 us

profile of v5, /device:TPU:1, one launch (start us, length us, event | category | flops | bytes accessed | tf_op | source)
XLA Modules:
  0.0 67.6 jit_solution(11984611967445401136)
XLA Ops:
  0.6 64.4 %shard_map.92 = (f32[8,8,288]{2,1,0:T(8,128)}, f32[4,8,288]{2,1,0:T(8,128)}, bf16[288,1152]{1,0:T(8,128)(2,1)}, bf16[288,1152]{1,0:T(8,128)(2,1)}, bf16[288,1152]{1,0:T(8,128)(2,1)}) custom-call(bf16[8,288]{1,0:T(8,128)(2,1)} %tok_h.1, bf16[8,288]{1,0:T(8,128)(2,1)} %cot_h.1, bf16[288,1152]{1,0:T(8,128)(2,1)} %gate_h.1, bf16[288,1152]{1,0:T(8,128)(2,1)} %up_h.1, ...), custom_call_target="tpu_custom_call" | custom-call | tf_op jit(solution)/shard_map/pallas_call | solution.py:367
  65.1 2.5 %shard_map.93 = (f32[8,288]{1,0:T(8,128)}, f32[8,288]{1,0:T(8,128)}, bf16[288,1152]{1,0:T(8,128)(2,1)}, bf16[288,1152]{1,0:T(8,128)(2,1)}, bf16[288,1152]{1,0:T(8,128)(2,1)}) custom-call(f32[8,8,288]{2,1,0:T(8,128)} %get-tuple-element.15.refs_0_, f32[4,8,288]{2,1,0:T(8,128)} %get-tuple-element.16.refs_1_, bf16[288,1152]{1,0:T(8,128)(2,1)} %get-tuple-element.17.refs_2_, ...), custom_call_target="tpu_custom_call" | custom-call | tf_op jit(solution)/shard_map/pallas_call | solution.py:377

commit v6 on v5

--- a/solution.py
+++ b/solution.py
@@ -42,9 +42,9 @@
     sizes,
     tok_h, cot_h, gate_h, up_h, down_h,
     SZ, SY, ggw_o, guw_o, gdw_o,
-    tok, cot, GV, UV, DV, WF, DF, WS, DS, XY, XO, XS, TK, CT, PB, RP, HB,
+    tok, cot, GV, UV, DV, WF, DF, WS, DS, XY, XZ, XO, XS, TK, CT, PB, RP, HB,
     AY, RY, AZ, RZ, BY, BZ, AF, ggw_v, guw_v, gdw_v,
-    ld_sem, wx_s, wx_r, py_s, py_r, pz_s, pz_r, xs_s, xs_r, rs_s, rs_r,
+    ld_sem, wx_s, wx_r, py_s, py_r, pz_s, pz_r, yz_s, yz_r, xs_s, xs_r, rs_s, rs_r,
     ag_s, ag_r, fw_s, fw_r, ay_s, ay_r, az_s, az_r, by_s, by_r, bz_s, bz_r, out_sem,
 ):
     NQ, NZ, NY = sizes
@@ -134,6 +134,11 @@
         send(XY.at[0], XY.at[j], py_s.at[j], py_r.at[j], dp, at_y(NY - j))
         for j in sorted(range(1, NY), key=lambda j: -min(j, NY - j))
     ]
+    pz = [None] * NZ
+    for p in range(slots, NZ):
+        pz[p] = send(
+            XY.at[0], XZ.at[p - slots], pz_s.at[p], pz_r.at[p], dp, at_z(NZ - order[p])
+        )
     for copy in loads:
         copy.wait()
     for h in range(2):
@@ -149,18 +154,20 @@
     lanes = XO.shape[2]
     whole, rest = F // lanes, F % lanes
     block_rows = NY * 2 * rows
-    for t in range(whole):
-        XO[0, t * block_rows : (t + 1) * block_rows] = XY[
-            :, :, t * lanes : (t + 1) * lanes
-        ].reshape(block_rows, lanes)
-    if rest:
-        XO[0, whole * block_rows :] = jnp.concatenate(
-            [XY[j, :, whole * lanes :] for j in range(NY)], axis=1
-        )
-    pz = [None] + [
-        send(XO.at[0], XO.at[p], pz_s.at[p], pz_r.at[p], dp, at_z(NZ - order[p]))
-        for p in range(1, NZ)
-    ]
+
+    def pack(blocks, at):
+        for t in range(whole):
+            XO[at, t * block_rows : (t + 1) * block_rows] = blocks[
+                :, :, t * lanes : (t + 1) * lanes
+            ].reshape(block_rows, lanes)
+        if rest:
+            XO[at, whole * block_rows :] = jnp.concatenate(
+                [blocks[j, :, whole * lanes :] for j in range(NY)], axis=1
+            )
+
+    pack(XY, 0)
+    for p in range(1, slots):
+        pz[p] = send(XO.at[0], XO.at[p], pz_s.at[p], pz_r.at[p], dp, at_z(NZ - order[p]))
     xs = [send(XO.at[0], XS.at[0], xs_s.at[0], xs_r.at[0], sib, mp)]
 
     def rows_of(ref, m):
@@ -176,10 +183,18 @@
             both[:, 1].reshape(part_rows, F).astype(BF16),
         )
 
+    for p in range(slots, NZ):
+        pz[p].wait_recv()
+    pack(XZ, slots)
+    for j in range(1, NY):
+        p = slots + j
+        pz[p] = send(XO.at[slots], XO.at[p], yz_s.at[j], yz_r.at[j], dp, at_y(NY - j))
+
     rs = []
     for m in range(2):
         for p in range(max(1, m * slots), (m + 1) * slots):
-            pz[p].wait_recv()
+            if p != slots:
+                pz[p].wait_recv()
             xs.append(send(XO.at[p], XS.at[p], xs_s.at[p], xs_r.at[p], sib, mp))
         t_own, c_own = rows_of(XO, m)
         TK[m] = t_own
@@ -239,12 +254,15 @@
         lo += dot_cols(acts[:, 2 * H :], DF[oc])
         lo = lo.reshape(slots, NY, rows, F)
         for j in range(NY):
-            AY[m, j] = lo[:, j].reshape(slots * rows, F).astype(BF16)
+            AY[m, j] = (lo[:, j] if m == 0 else lo[j]).reshape(slots * rows, F).astype(BF16)
         for j in range(1, NY):
             ay.append(send(AY.at[m, j], RY.at[m, j], ay_s.at[m, j], ay_r.at[m, j], dp, at_y(j)))
         RY[m, 0] = AY[m, 0]
         gi += dot_cols(acts[:, : 2 * H], WF[oc])
-        AZ[m * slots : (m + 1) * slots] = gi.astype(BF16).reshape(slots, NY * rows, F)
+        gi = gi.reshape(slots, NY, rows, F)
+        for p in range(slots):
+            terms = gi[p] if m == 0 else gi[:, p]
+            AZ[m * slots + p] = terms.reshape(NY * rows, F).astype(BF16)
         for p in range(max(1, m * slots), (m + 1) * slots):
             az.append(send(AZ.at[p], RZ.at[p], az_s.at[p], az_r.at[p], dp, at_z(order[p])))
         if m == 0:
@@ -345,7 +363,7 @@
             ((rows, F), BF16), ((rows, F), BF16),
             ((F, U), BF16), ((F, U), BF16), ((F, U), BF16),
             ((2, F, U), BF16), ((2, F, H), BF16), ((F, U), BF16), ((F, H), BF16),
-            ((NY, 2 * rows, F), BF16), ((NZ, packed, LANES), BF16), ((NZ, packed, LANES), BF16),
+            ((NY, 2 * rows, F), BF16), ((NY, 2 * rows, F), BF16), ((NZ, packed, LANES), BF16), ((NZ, packed, LANES), BF16),
             ((2, T // 2, F), BF16), ((2, T // 2, F), BF16),
             ((2, NQ, R, 3 * H), BF16), ((2, NQ, R, 3 * H), BF16), ((2, 2, NQ, R, 3 * H), BF16),
             ((2, NY, NZ // 2 * rows, F), BF16), ((2, NY, NZ // 2 * rows, F), BF16),
@@ -353,7 +371,7 @@
             ((NY, rows, F), F32), ((NZ, rows, F), F32), ((T, U), BF16),
             ((F, U), BF16), ((F, U), BF16), ((F, U), BF16),
         ]
-        sems = [(5,), (2,), (2,), (NY,), (NY,), (NZ,), (NZ,), (NZ,), (NZ,), (2, NQ), (2, NQ),
+        sems = [(5,), (2,), (2,), (NY,), (NY,), (NZ,), (NZ,), (NY,), (NY,), (NZ,), (NZ,), (2, NQ), (2, NQ),
                 (2, NQ), (2, NQ), (2, NQ), (2, NQ), (2, NY), (2, NY), (NZ,), (NZ,),
                 (NY,), (NY,), (NZ,), (NZ,), (5,)]
         shapes = (

time: 67.8 us -> 67 us (0.988)
  Pallas kernels: 67 us -> 66.2 us
    pallas_call x1, Pallas kernels: 64.4 us -> 63.7 us  [local(): pl.pallas_call(functools.partial(kernel, (NQ, NZ, NY)), out_shape=terms +...]
where the time goes in v6:
time: 67 us; the launch traced here: 66.9 us
  Pallas kernels  66.2 us (99%)
    pallas_call x1, Pallas kernels, local(): pl.pallas_call(functools.partial(kernel, (NQ, NZ, NY)), out_shape=terms +...  63.7 us
    pallas_call x1, Pallas kernels, local(): pl.pallas_call(closing_kernel, out_shape=shapes, in_specs=[anywhere] * 5,...  2.54 us

profile of v6, /device:TPU:1, one launch (start us, length us, event | category | flops | bytes accessed | tf_op | source)
XLA Modules:
  0.0 66.9 jit_solution(14829617079294961851)
XLA Ops:
  0.6 63.7 %shard_map.92 = (f32[8,8,288]{2,1,0:T(8,128)}, f32[4,8,288]{2,1,0:T(8,128)}, bf16[288,1152]{1,0:T(8,128)(2,1)}, bf16[288,1152]{1,0:T(8,128)(2,1)}, bf16[288,1152]{1,0:T(8,128)(2,1)}) custom-call(bf16[8,288]{1,0:T(8,128)(2,1)} %tok_h.1, bf16[8,288]{1,0:T(8,128)(2,1)} %cot_h.1, bf16[288,1152]{1,0:T(8,128)(2,1)} %gate_h.1, bf16[288,1152]{1,0:T(8,128)(2,1)} %up_h.1, ...), custom_call_target="tpu_custom_call" | custom-call | tf_op jit(solution)/shard_map/pallas_call | solution.py:385
  64.3 2.5 %shard_map.93 = (f32[8,288]{1,0:T(8,128)}, f32[8,288]{1,0:T(8,128)}, bf16[288,1152]{1,0:T(8,128)(2,1)}, bf16[288,1152]{1,0:T(8,128)(2,1)}, bf16[288,1152]{1,0:T(8,128)(2,1)}) custom-call(f32[8,8,288]{2,1,0:T(8,128)} %get-tuple-element.15.refs_0_, f32[4,8,288]{2,1,0:T(8,128)} %get-tuple-element.16.refs_1_, bf16[288,1152]{1,0:T(8,128)(2,1)} %get-tuple-element.17.refs_2_, ...), custom_call_target="tpu_custom_call" | custom-call | tf_op jit(solution)/shard_map/pallas_call | solution.py:395
